TPU v7x, 1024 devices: a whole 4x4x32 slice. The times are simulated.
1024 devices in a mesh: node: 32 (over z), inner: 4 (over y), rep: 8 (over x, core).
Axes of the slice: x: 4, y: 4, z: 32, core: 2. Of those that a mesh axis runs over, the one named last changes fastest.
Arguments:
- tokens: bfloat16 [16384, 1024], P(('node', 'inner', 'rep')), may hold values from -6 to 6
- out_grad: bfloat16 [16384, 1024], P(('node', 'inner', 'rep')), may hold values from -6 to 6
- expert_ids: int32 [16384, 10], P(('node', 'inner', 'rep')), may hold values from 0 to 255, as said below
- route_weight: float32 [16384, 10], P(('node', 'inner', 'rep')), may hold values from 0.1 to 0.6
- gate_weight: bfloat16 [256, 1024, 256], P(('node', 'inner')), may hold values from -0.1875 to 0.1875
- up_weight: bfloat16 [256, 1024, 256], P(('node', 'inner')), may hold values from -0.1875 to 0.1875
- down_weight: bfloat16 [256, 256, 1024], P(('node', 'inner')), may hold values from -0.375 to 0.375
Outputs:
- mixed: bfloat16 [16384, 1024], P(('node', 'inner', 'rep'))
- grad_tokens: bfloat16 [16384, 1024], P(('node', 'inner', 'rep'))
- grad_route: float32 [16384, 10], P(('node', 'inner', 'rep'))
- grad_gate: bfloat16 [256, 1024, 256], P(('node', 'inner'), 'rep')
- grad_up: bfloat16 [256, 1024, 256], P(('node', 'inner'), 'rep')
- grad_down: bfloat16 [256, 256, 1024], P(('node', 'inner'), None, 'rep')
Inputs may be any that keep to these rules, and one draw needn't show every extreme that they name: `expert_ids`: each token names 10 different experts. Expert e is held in every rep group by the device whose index over node+inner is e // 2. The 160 entries of one device name experts of any one device at most 2 times and any one expert at most 1 times; every device names some device exactly 2 times and some expert exactly 1 times.
All inputs are finite; a program needn't handle non-finite values.
Results may differ from a plain program's by a relative error of at most 0.017.
Values may be sent and summed in bfloat16 or wider, within the bound.
A program may use at most 32 MiB of HBM per device.

v0:
```python
import jax
import jax.numpy as jnp
from jax import lax
from jax.sharding import PartitionSpec as P


def per_device(tokens, out_grad, expert_ids, route_weight, gate_weight, up_weight, down_weight):
    token_count, model_width = tokens.shape
    top_count = expert_ids.shape[1]
    local_experts = gate_weight.shape[0]
    node_count = lax.axis_size("node")
    inner_count = lax.axis_size("inner")
    dest_count = node_count * inner_count
    row_count = token_count * top_count
    capacity = max(2, -(-row_count // dest_count))
    per_expert = (capacity + 1) // 2
    expert_total = dest_count * local_experts
    slot_count = expert_total * per_expert
    flat_ids = expert_ids.reshape(row_count)
    id_onehot = (flat_ids[:, None] == jnp.arange(expert_total, dtype=jnp.int32)[None, :]).astype(
        jnp.int32
    )
    earlier_count = jnp.cumsum(id_onehot, axis=0) - id_onehot
    rank_within = jnp.sum(earlier_count * id_onehot, axis=1)
    slot_index = flat_ids * per_expert + rank_within
    placement = (slot_index[:, None] == jnp.arange(slot_count, dtype=jnp.int32)[None, :]).astype(
        jnp.bfloat16
    )
    token_rows = jnp.repeat(tokens, top_count, axis=0)
    grad_rows = jnp.repeat(out_grad, top_count, axis=0)
    scaled_rows = (route_weight.reshape(row_count, 1) * grad_rows.astype(jnp.float32)).astype(
        jnp.bfloat16
    )
    send_tokens = jnp.einsum(
        "rs,rd->sd", placement, token_rows, preferred_element_type=jnp.float32
    ).astype(jnp.bfloat16)
    send_grads = jnp.einsum(
        "rs,rd->sd", placement, scaled_rows, preferred_element_type=jnp.float32
    ).astype(jnp.bfloat16)
    block_shape = (node_count, inner_count, local_experts, per_expert, model_width)
    got_tokens, got_grads = (
        lax.all_to_all(
            lax.all_to_all(
                send_tokens.reshape(block_shape), "node", split_axis=0, concat_axis=0, tiled=True
            ),
            "inner",
            split_axis=1,
            concat_axis=1,
            tiled=True,
        ),
        lax.all_to_all(
            lax.all_to_all(
                send_grads.reshape(block_shape), "node", split_axis=0, concat_axis=0, tiled=True
            ),
            "inner",
            split_axis=1,
            concat_axis=1,
            tiled=True,
        ),
    )
    served_shape = (dest_count, local_experts, per_expert, model_width)
    served = got_tokens.reshape(served_shape)
    served_grads = got_grads.reshape(served_shape)
    gate_pre = jnp.einsum("nesd,edf->nesf", served, gate_weight, preferred_element_type=jnp.float32)
    up_pre = jnp.einsum("nesd,edf->nesf", served, up_weight, preferred_element_type=jnp.float32)
    gate_sig = jax.nn.sigmoid(gate_pre)
    silu_value = gate_pre * gate_sig
    activations = (silu_value * up_pre).astype(jnp.bfloat16)
    expert_out = jnp.einsum(
        "nesf,efd->nesd", activations, down_weight, preferred_element_type=jnp.float32
    ).astype(jnp.bfloat16)
    act_grad = jnp.einsum(
        "nesd,efd->nesf", served_grads, down_weight, preferred_element_type=jnp.float32
    )
    up_grads = (act_grad * silu_value).astype(jnp.bfloat16)
    gate_grads = (act_grad * up_pre * (gate_sig * (1.0 + gate_pre * (1.0 - gate_sig)))).astype(
        jnp.bfloat16
    )
    back_sum = jnp.einsum(
        "nesf,edf->nesd", gate_grads, gate_weight, preferred_element_type=jnp.float32
    )
    back_sum = back_sum + jnp.einsum(
        "nesf,edf->nesd", up_grads, up_weight, preferred_element_type=jnp.float32
    )
    token_back = back_sum.astype(jnp.bfloat16)
    ret_out, ret_back = (
        lax.all_to_all(
            lax.all_to_all(
                expert_out.reshape(block_shape), "node", split_axis=0, concat_axis=0, tiled=True
            ),
            "inner",
            split_axis=1,
            concat_axis=1,
            tiled=True,
        ),
        lax.all_to_all(
            lax.all_to_all(
                token_back.reshape(block_shape), "node", split_axis=0, concat_axis=0, tiled=True
            ),
            "inner",
            split_axis=1,
            concat_axis=1,
            tiled=True,
        ),
    )
    out_rows = jnp.einsum(
        "rs,sd->rd",
        placement,
        ret_out.reshape(slot_count, model_width),
        preferred_element_type=jnp.float32,
    ).reshape(token_count, top_count, model_width)
    mixed = jnp.sum(route_weight[:, :, None] * out_rows, axis=1).astype(jnp.bfloat16)
    grad_route = jnp.sum(out_rows * out_grad[:, None, :].astype(jnp.float32), axis=2)
    token_place = jnp.sum(placement.reshape(token_count, top_count, slot_count), axis=1)
    grad_tokens = jnp.dot(
        token_place, ret_back.reshape(slot_count, model_width), preferred_element_type=jnp.float32
    ).astype(jnp.bfloat16)
    term_gate = jnp.einsum("nesd,nesf->edf", served, gate_grads, preferred_element_type=jnp.float32)
    term_up = jnp.einsum("nesd,nesf->edf", served, up_grads, preferred_element_type=jnp.float32)
    term_down = jnp.einsum(
        "nesf,nesd->efd", activations, served_grads, preferred_element_type=jnp.float32
    )
    sum_gate, sum_up, sum_down = (
        lax.psum_scatter(
            term_gate.astype(jnp.bfloat16), "rep", scatter_dimension=1, tiled=True
        ).astype(jnp.float32),
        lax.psum_scatter(
            term_up.astype(jnp.bfloat16), "rep", scatter_dimension=1, tiled=True
        ).astype(jnp.float32),
        lax.psum_scatter(
            term_down.astype(jnp.bfloat16), "rep", scatter_dimension=2, tiled=True
        ).astype(jnp.float32),
    )
    return (
        mixed,
        grad_tokens,
        grad_route,
        sum_gate.astype(jnp.bfloat16),
        sum_up.astype(jnp.bfloat16),
        sum_down.astype(jnp.bfloat16),
    )


def solution(mesh):
    return jax.shard_map(
        per_device,
        mesh=mesh,
        in_specs=(
            P(("node", "inner", "rep"), None),
            P(("node", "inner", "rep"), None),
            P(("node", "inner", "rep"), None),
            P(("node", "inner", "rep"), None),
            P(("node", "inner"), None, None),
            P(("node", "inner"), None, None),
            P(("node", "inner"), None, None),
        ),
        out_specs=(
            P(("node", "inner", "rep"), None),
            P(("node", "inner", "rep"), None),
            P(("node", "inner", "rep"), None),
            P(("node", "inner"), "rep", None),
            P(("node", "inner"), "rep", None),
            P(("node", "inner"), None, "rep"),
        ),
        check_vma=False,
    )
```

profile of v0, /device:TPU:7, one launch (start us, length us, event | category | flops | bytes accessed | tf_op | source)
XLA Modules:
  0.0 389.8 jit_solution(1464157238455935566)
XLA Ops:
  10.5 28.4 %all-to-all-start = ((bf16[32,4,2,1,1024]{4,2,1,3,0:T(2,128)(2,1)}), bf16[32,4,2,1,1024]{4,2,1,3,0:T(2,128)(2,1)S(1)}, u32[]{:S(2)}, u32[]{:S(2)}) async-start(bf16[32,4,2,1,1024]{4,2,1,3,0:T(2,128)(2,1)} %bitcast.5), calls=%async_computation | async-start | bytes 1048576 | tf_op jit(solution)/shard_map/all_to_all | solution.py:43
  41.3 61.9 %all-to-all-done = bf16[32,4,2,1,1024]{4,2,1,3,0:T(2,128)(2,1)S(1)} async-done(((bf16[32,4,2,1,1024]{4,2,1,3,0:T(2,128)(2,1)}), bf16[32,4,2,1,1024]{4,2,1,3,0:T(2,128)(2,1)S(1)}, u32[]{:S(2)}, u32[]{:S(2)}) %all-to-all-start) | async-done | bytes 524320 | tf_op jit(solution)/shard_map/all_to_all | solution.py:43
  103.3 3.9 all-to-all-start.4
  108.3 63.2 %all-to-all-done.4 = bf16[32,4,2,1,1024]{4,2,1,3,0:T(2,128)(2,1)S(1)} async-done(((bf16[32,4,2,1,1024]{4,2,1,3,0:T(2,128)(2,1)}), bf16[32,4,2,1,1024]{4,2,1,3,0:T(2,128)(2,1)S(1)}, u32[]{:S(2)}, u32[]{:S(2)}) %all-to-all-start.4) | async-done | bytes 524320 | tf_op jit(solution)/shard_map/all_to_all | solution.py:52
  171.6 4.2 %all-to-all-start.1 = ((bf16[32,4,2,1,1024]{4,2,0,3,1:T(2,128)(2,1)}), bf16[32,4,2,1,1024]{4,2,0,3,1:T(2,128)(2,1)S(1)}, u32[]{:S(2)}, u32[]{:S(2)}) async-start(bf16[32,4,2,1,1024]{4,2,0,3,1:T(2,128)(2,1)} %copy.59), calls=%async_computation.1 | async-start | bytes 1048576 | tf_op jit(solution)/shard_map/all_to_all | solution.py:42
  176.9 6.0 %all-to-all-done.1 = bf16[32,4,2,1,1024]{4,2,0,3,1:T(2,128)(2,1)S(1)} async-done(((bf16[32,4,2,1,1024]{4,2,0,3,1:T(2,128)(2,1)}), bf16[32,4,2,1,1024]{4,2,0,3,1:T(2,128)(2,1)S(1)}, u32[]{:S(2)}, u32[]{:S(2)}) %all-to-all-start.1) | async-done | bytes 524320 | tf_op jit(solution)/shard_map/all_to_all | solution.py:42
  182.9 4.1 %all-to-all-start.5 = ((bf16[32,4,2,1,1024]{4,2,0,3,1:T(2,128)(2,1)}), bf16[32,4,2,1,1024]{4,2,0,3,1:T(2,128)(2,1)}, u32[]{:S(2)}, u32[]{:S(2)}) async-start(bf16[32,4,2,1,1024]{4,2,0,3,1:T(2,128)(2,1)} %copy.67), calls=%async_computation.5 | async-start | bytes 1048576 | tf_op jit(solution)/shard_map/all_to_all | solution.py:51
  187.6 6.4 %all-to-all-done.5 = bf16[32,4,2,1,1024]{4,2,0,3,1:T(2,128)(2,1)} async-done(((bf16[32,4,2,1,1024]{4,2,0,3,1:T(2,128)(2,1)}), bf16[32,4,2,1,1024]{4,2,0,3,1:T(2,128)(2,1)}, u32[]{:S(2)}, u32[]{:S(2)}) %all-to-all-start.5) | async-done | bytes 524320 | tf_op jit(solution)/shard_map/all_to_all | solution.py:51
  194.0 2.2 copy.68
  200.5 1.4 copy.79
  201.9 5.4 %all-to-all-start.6 = ((bf16[32,4,2,1,1024]{4,2,1,3,0:T(2,128)(2,1)}), bf16[32,4,2,1,1024]{4,2,1,3,0:T(2,128)(2,1)S(1)}, u32[]{:S(2)}, u32[]{:S(2)}) async-start(bf16[32,4,2,1,1024]{4,2,1,3,0:T(2,128)(2,1)} %bitcast.31), calls=%async_computation.6 | async-start | bytes 1048576 | tf_op jit(solution)/shard_map/all_to_all | solution.py:97
  207.3 1.4 convolution_convert_fusion
  208.8 2.5 copy.80
  214.8 1.2 reshape.139
  217.1 48.7 %all-to-all-done.6 = bf16[32,4,2,1,1024]{4,2,1,3,0:T(2,128)(2,1)S(1)} async-done(((bf16[32,4,2,1,1024]{4,2,1,3,0:T(2,128)(2,1)}), bf16[32,4,2,1,1024]{4,2,1,3,0:T(2,128)(2,1)S(1)}, u32[]{:S(2)}, u32[]{:S(2)}) %all-to-all-start.6) | async-done | bytes 524320 | tf_op jit(solution)/shard_map/all_to_all | solution.py:97
  265.8 7.9 %all-to-all-start.2 = ((bf16[32,4,2,1,1024]{4,1,2,3,0:T(4,128)(2,1)}), bf16[32,4,2,1,1024]{4,1,2,3,0:T(4,128)(2,1)S(1)}, u32[]{:S(2)}, u32[]{:S(2)}) async-start(bf16[32,4,2,1,1024]{4,1,2,3,0:T(4,128)(2,1)} %copy.61), calls=%async_computation.2 | async-start | bytes 1048576 | tf_op jit(solution)/shard_map/all_to_all | solution.py:88
  273.8 1.5 convolution_convert_fusion.2
  275.3 1.5 convolution_convert_fusion.1
  278.0 54.2 %all-to-all-done.2 = bf16[32,4,2,1,1024]{4,1,2,3,0:T(4,128)(2,1)S(1)} async-done(((bf16[32,4,2,1,1024]{4,1,2,3,0:T(4,128)(2,1)}), bf16[32,4,2,1,1024]{4,1,2,3,0:T(4,128)(2,1)S(1)}, u32[]{:S(2)}, u32[]{:S(2)}) %all-to-all-start.2) | async-done | bytes 524320 | tf_op jit(solution)/shard_map/all_to_all | solution.py:88
  332.2 3.5 all-to-all-start.7
  336.8 5.8 %all-to-all-done.7 = bf16[32,4,2,1,1024]{4,2,0,3,1:T(2,128)(2,1)S(1)} async-done(((bf16[32,4,2,1,1024]{4,2,0,3,1:T(2,128)(2,1)}), bf16[32,4,2,1,1024]{4,2,0,3,1:T(2,128)(2,1)S(1)}, u32[]{:S(2)}, u32[]{:S(2)}) %all-to-all-start.7) | async-done | bytes 524320 | tf_op jit(solution)/shard_map/all_to_all | solution.py:96
  342.6 3.5 all-to-all-start.3
  348.9 4.3 %all-to-all-done.3 = bf16[32,4,2,1,1024]{4,0,2,3,1:T(8,128)(2,1)S(1)} async-done(((bf16[32,4,2,1,1024]{4,0,2,3,1:T(8,128)(2,1)}), bf16[32,4,2,1,1024]{4,0,2,3,1:T(8,128)(2,1)S(1)}, u32[]{:S(2)}, u32[]{:S(2)}) %all-to-all-start.3) | async-done | bytes 524320 | tf_op jit(solution)/shard_map/all_to_all | solution.py:87
  356.3 27.0 %reduce-scatter.8.cloned.1.call-done = bf16[2,128,256]{2,1,0:T(8,128)(2,1)} async-done(((bf16[2,1024,256]{2,1,0:T(8,128)(2,1)}), bf16[2,128,256]{2,1,0:T(8,128)(2,1)}) %reduce-scatter.8.cloned.1.call-update) | async-done | bytes 131088 | tf_op jit(solution)/shard_map/reduce_scatter | solution.py:127
  (77 shorter events, 25.6 us)
Async XLA Ops:
  7.2 192.0 %copy-start = (bf16[2,1024,256]{2,1,0:T(8,128)(2,1)S(1)}, bf16[2,1024,256]{2,1,0:T(8,128)(2,1)}, u32[]{:S(2)}) copy-start(bf16[2,1024,256]{2,1,0:T(8,128)(2,1)} %param.11) | copy-start | bytes 3145732
  8.2 0.8 copy-start.6
  9.5 29.5 %copy-start.4 = (bf16[16,1024]{1,0:T(8,128)(2,1)S(1)}, bf16[16,1024]{1,0:T(8,128)(2,1)}, u32[]{:S(2)}) copy-start(bf16[16,1024]{1,0:T(8,128)(2,1)} %param.8) | copy-start | bytes 98308
  10.5 92.7 %all-to-all-start = ((bf16[32,4,2,1,1024]{4,2,1,3,0:T(2,128)(2,1)}), bf16[32,4,2,1,1024]{4,2,1,3,0:T(2,128)(2,1)S(1)}, u32[]{:S(2)}, u32[]{:S(2)}) async-start(bf16[32,4,2,1,1024]{4,2,1,3,0:T(2,128)(2,1)} %bitcast.5), calls=%async_computation | async-start | bytes 1048576 | tf_op jit(solution)/shard_map/all_to_all | solution.py:43
  39.1 0.7 copy-start.8
  103.3 68.3 %all-to-all-start.4 = ((bf16[32,4,2,1,1024]{4,2,1,3,0:T(2,128)(2,1)}), bf16[32,4,2,1,1024]{4,2,1,3,0:T(2,128)(2,1)S(1)}, u32[]{:S(2)}, u32[]{:S(2)}) async-start(bf16[32,4,2,1,1024]{4,2,1,3,0:T(2,128)(2,1)} %bitcast.18), calls=%async_computation.4 | async-start | bytes 1048576 | tf_op jit(solution)/shard_map/all_to_all | solution.py:52
  171.6 11.3 %all-to-all-start.1 = ((bf16[32,4,2,1,1024]{4,2,0,3,1:T(2,128)(2,1)}), bf16[32,4,2,1,1024]{4,2,0,3,1:T(2,128)(2,1)S(1)}, u32[]{:S(2)}, u32[]{:S(2)}) async-start(bf16[32,4,2,1,1024]{4,2,0,3,1:T(2,128)(2,1)} %copy.59), calls=%async_computation.1 | async-start | bytes 1048576 | tf_op jit(solution)/shard_map/all_to_all | solution.py:42
  182.9 11.1 %all-to-all-start.5 = ((bf16[32,4,2,1,1024]{4,2,0,3,1:T(2,128)(2,1)}), bf16[32,4,2,1,1024]{4,2,0,3,1:T(2,128)(2,1)}, u32[]{:S(2)}, u32[]{:S(2)}) async-start(bf16[32,4,2,1,1024]{4,2,0,3,1:T(2,128)(2,1)} %copy.67), calls=%async_computation.5 | async-start | bytes 1048576 | tf_op jit(solution)/shard_map/all_to_all | solution.py:51
  187.5 9.8 %copy-start.1 = (bf16[2,1024,256]{2,1,0:T(8,128)(2,1)S(1)}, bf16[2,1024,256]{2,1,0:T(8,128)(2,1)}, u32[]{:S(2)}) copy-start(bf16[2,1024,256]{2,1,0:T(8,128)(2,1)} %param.12) | copy-start | bytes 3145732
  197.4 1.2 copy-start.2
  201.9 63.9 %all-to-all-start.6 = ((bf16[32,4,2,1,1024]{4,2,1,3,0:T(2,128)(2,1)}), bf16[32,4,2,1,1024]{4,2,1,3,0:T(2,128)(2,1)S(1)}, u32[]{:S(2)}, u32[]{:S(2)}) async-start(bf16[32,4,2,1,1024]{4,2,1,3,0:T(2,128)(2,1)} %bitcast.31), calls=%async_computation.6 | async-start | bytes 1048576 | tf_op jit(solution)/shard_map/all_to_all | solution.py:97
  207.3 139.2 %reduce-scatter.10.cloned.1.call-start = ((), (), s32[]{:S(2)}) async-start(), calls=%async_computation.13 | async-start | bytes 1179648
  212.5 1.2 copy-start.3
  265.8 66.4 %all-to-all-start.2 = ((bf16[32,4,2,1,1024]{4,1,2,3,0:T(4,128)(2,1)}), bf16[32,4,2,1,1024]{4,1,2,3,0:T(4,128)(2,1)S(1)}, u32[]{:S(2)}, u32[]{:S(2)}) async-start(bf16[32,4,2,1,1024]{4,1,2,3,0:T(4,128)(2,1)} %copy.61), calls=%async_computation.2 | async-start | bytes 1048576 | tf_op jit(solution)/shard_map/all_to_all | solution.py:88
  273.7 82.6 %reduce-scatter.6.cloned.1.call-start = ((), (), s32[]{:S(2)}) async-start(), calls=%async_computation.11 | async-start | bytes 1179648 | tf_op jit(solution)/shard_map/reduce_scatter | solution.py:124
  275.3 108.0 %reduce-scatter.8.cloned.1.call-start = ((), (), s32[]{:S(2)}) async-start(), calls=%async_computation.12 | async-start | bytes 1179648 | tf_op jit(solution)/shard_map/reduce_scatter | solution.py:127
  332.2 10.4 %all-to-all-start.7 = ((bf16[32,4,2,1,1024]{4,2,0,3,1:T(2,128)(2,1)}), bf16[32,4,2,1,1024]{4,2,0,3,1:T(2,128)(2,1)S(1)}, u32[]{:S(2)}, u32[]{:S(2)}) async-start(bf16[32,4,2,1,1024]{4,2,0,3,1:T(2,128)(2,1)} %copy.70), calls=%async_computation.7 | async-start | bytes 1048576 | tf_op jit(solution)/shard_map/all_to_all | solution.py:96
  335.7 10.5 %copy-start.5 = (bf16[16,1024]{1,0:T(8,128)(2,1)S(1)}, bf16[16,1024]{1,0:T(8,128)(2,1)}, u32[]{:S(2)}) copy-start(bf16[16,1024]{1,0:T(8,128)(2,1)} %param.8) | copy-start | bytes 98308
  335.7 10.6 %copy-start.7 = (s32[16,10]{1,0:T(8,128)S(1)}, s32[16,10]{1,0:T(8,128)}, u32[]{:S(2)}) copy-start(s32[16,10]{1,0:T(8,128)} %param.9) | copy-start | bytes 1924
  342.6 10.6 %all-to-all-start.3 = ((bf16[32,4,2,1,1024]{4,0,2,3,1:T(8,128)(2,1)}), bf16[32,4,2,1,1024]{4,0,2,3,1:T(8,128)(2,1)S(1)}, u32[]{:S(2)}, u32[]{:S(2)}) async-start(bf16[32,4,2,1,1024]{4,0,2,3,1:T(8,128)(2,1)} %copy.62), calls=%async_computation.3 | async-start | bytes 1048576 | tf_op jit(solution)/shard_map/all_to_all | solution.py:87
Sparse Core Ops, SparseCore 0:
  212.6 52.0 reduce-scatter.9
  278.5 52.1 reduce-scatter.5
  334.7 48.5 reduce-scatter.7
where the time goes:
time: 391 us; the launch traced here: 390 us
  waiting for transfers between devices  278 us (71%)
  starting transfers between devices  61 us (16%)
  local copies, waits for them, and re-layouts  26.2 us (7%)
  between operations  14.1 us (4%)
  matrix products  10.2 us (3%)
    all_to_all x1, waiting for transfers between devices, per_device(): lax.all_to_all(send_grads.reshape(block_shape), 'node', split_axis=0, con...  63.2 us
    all_to_all x1, waiting for transfers between devices, per_device(): lax.all_to_all(send_tokens.reshape(block_shape), 'node', split_axis=0, co...  61.9 us
    all_to_all x1, waiting for transfers between devices, per_device(): lax.all_to_all(expert_out.reshape(block_shape), 'node', split_axis=0, con...  54.2 us
    all_to_all x1, waiting for transfers between devices, per_device(): lax.all_to_all(token_back.reshape(block_shape), 'node', split_axis=0, con...  48.7 us
    all_to_all x1, starting transfers between devices, per_device(): lax.all_to_all(send_tokens.reshape(block_shape), 'node', split_axis=0, co...  28.4 us
    reduce_scatter x1, waiting for transfers between devices, per_device(): lax.psum_scatter(term_up.astype(jnp.bfloat16), 'rep', scatter_dimension=1...  27 us
    unnamed x25, local copies, waits for them, and re-layouts  9.1 us
    all_to_all x1, starting transfers between devices, per_device(): lax.all_to_all(expert_out.reshape(block_shape), 'node', split_axis=0, con...  7.87 us
  transfers between devices with their start and end apart: 11, of which 9 were waited for; matrix products, arithmetic and copies ran while one was open for 6% of the time, Pallas kernels for 0%

commit v1 on v0

v1 whole, which is shorter than its diff:
```python
import jax
import jax.numpy as jnp
from jax import lax
from jax.sharding import PartitionSpec as P

BF16 = jnp.bfloat16
F32 = jnp.float32
LANES = 128


def split_weight(weight):
    high = lax.reduce_precision(weight, 8, 7)
    rest = weight - high
    middle = lax.reduce_precision(rest, 8, 7)
    return high, middle, rest - middle


def per_device(tokens, out_grad, expert_ids, route_weight, gate_weight, up_weight, down_weight):
    token_count, width = tokens.shape
    top = expert_ids.shape[1]
    local = gate_weight.shape[0]
    nodes = lax.axis_size("node")
    inners = lax.axis_size("inner")
    node = lax.axis_index("node")
    inner = lax.axis_index("inner")
    meta = jnp.concatenate(
        (expert_ids.astype(F32),) + split_weight(route_weight)
        + (jnp.zeros((token_count, LANES - 4 * top), F32),),
        axis=1,
    ).astype(BF16)
    payload = jnp.concatenate((tokens, out_grad, meta), axis=1)
    gathered = lax.all_gather(payload, "node", axis=0, tiled=True)
    ids = gathered[:, 2 * width : 2 * width + top].astype(F32)
    plane = (node * (inners * local) + jnp.arange(inners * local, dtype=jnp.int32)).astype(F32)
    chosen = jnp.any(ids[None] == plane[:, None, None], axis=2).astype(BF16)
    pick = (
        chosen.reshape(inners * local, 1, nodes, token_count)
        * jnp.eye(nodes, dtype=BF16)[None, :, :, None]
    ).reshape(inners * local * nodes, nodes * token_count)
    slots = jnp.dot(pick, gathered, preferred_element_type=F32).astype(BF16)
    served = lax.all_to_all(
        slots.reshape(inners, local, nodes, -1), "inner", split_axis=0, concat_axis=0, tiled=True
    )
    served = served.transpose(1, 0, 2, 3).reshape(local, inners * nodes, -1)
    rows = served[:, :, :width]
    grads = served[:, :, width : 2 * width].astype(F32)
    extra = served[:, :, 2 * width :].astype(F32)
    mine = ((node * inners + inner) * local + jnp.arange(local, dtype=jnp.int32)).astype(F32)
    is_mine = (extra[:, :, :top] == mine[:, None, None]).astype(F32)
    weights = (
        extra[:, :, top : 2 * top] + extra[:, :, 2 * top : 3 * top] + extra[:, :, 3 * top : 4 * top]
    )
    weight = jnp.sum(weights * is_mine, axis=2, keepdims=True)
    scaled = (weight * grads).astype(BF16)
    gate_pre = jnp.einsum("esd,edf->esf", rows, gate_weight, preferred_element_type=F32)
    up_pre = jnp.einsum("esd,edf->esf", rows, up_weight, preferred_element_type=F32)
    gate_sig = jax.nn.sigmoid(gate_pre)
    silu = gate_pre * gate_sig
    activation = (silu * up_pre).astype(BF16)
    expert_out = jnp.einsum("esf,efd->esd", activation, down_weight, preferred_element_type=F32)
    act_grad = jnp.einsum("esd,efd->esf", scaled, down_weight, preferred_element_type=F32)
    up_grad = (act_grad * silu).astype(BF16)
    gate_grad = (act_grad * up_pre * (gate_sig * (1.0 + gate_pre * (1.0 - gate_sig)))).astype(BF16)
    back = jnp.einsum("esf,edf->esd", gate_grad, gate_weight, preferred_element_type=F32)
    back = back + jnp.einsum("esf,edf->esd", up_grad, up_weight, preferred_element_type=F32)
    route = jnp.sum(grads * expert_out, axis=2, keepdims=True) * is_mine
    route = jnp.pad(route, ((0, 0), (0, 0), (0, LANES - top)))
    answer = jnp.concatenate((weight * expert_out, back, route), axis=2).astype(BF16)
    answer = answer.reshape(local, inners, nodes, -1).transpose(1, 0, 2, 3)
    answer = lax.all_to_all(answer, "inner", split_axis=0, concat_axis=0, tiled=True)
    partial = jnp.einsum(
        "st,sd->td",
        pick,
        answer.reshape(inners * local * nodes, -1),
        preferred_element_type=F32,
    ).astype(BF16)
    total = lax.psum_scatter(partial, "node", scatter_dimension=0, tiled=True)
    term_gate = jnp.einsum("esd,esf->edf", rows, gate_grad, preferred_element_type=F32)
    term_up = jnp.einsum("esd,esf->edf", rows, up_grad, preferred_element_type=F32)
    term_down = jnp.einsum("esf,esd->efd", activation, scaled, preferred_element_type=F32)
    sum_gate = lax.psum_scatter(term_gate.astype(BF16), "rep", scatter_dimension=1, tiled=True)
    sum_up = lax.psum_scatter(term_up.astype(BF16), "rep", scatter_dimension=1, tiled=True)
    sum_down = lax.psum_scatter(term_down.astype(BF16), "rep", scatter_dimension=2, tiled=True)
    return (
        total[:, :width],
        total[:, width : 2 * width],
        total[:, 2 * width : 2 * width + top].astype(F32),
        sum_gate,
        sum_up,
        sum_down,
    )


def solution(mesh):
    split = P(("node", "inner", "rep"), None)
    held = P(("node", "inner"), None, None)
    return jax.shard_map(
        per_device,
        mesh=mesh,
        in_specs=(split,) * 4 + (held,) * 3,
        out_specs=(split,) * 3
        + (P(("node", "inner"), "rep", None),) * 2
        + (P(("node", "inner"), None, "rep"),),
        check_vma=False,
    )
```

time: 391 us -> 482 us (1.23)
  waiting for transfers between devices: 278 us -> 416 us
  starting transfers between devices: 61 us -> 4.17 us
  blocking collectives: 0 us -> 12.6 us
  local copies, waits for them, and re-layouts: 26.2 us -> 15.2 us
  matrix products: 10.2 us -> 15.1 us
    all_to_all x8 -> x1, waiting for transfers between devices: 251 us -> 10.1 us  [per_device(): lax.all_to_all(slots.reshape(inners, local, nodes, -1), 'inner', split_ax...]
    reduce_scatter x2 -> x3, waiting for transfers between devices: 27 us -> 238 us  [the longest x1 117 us: per_device(): total = lax.psum_scatter(partial, 'node', scatter_dimension=0, tiled=True)]
    all_gather x0 -> x1, waiting for transfers between devices: none -> 128 us  [per_device(): gathered = lax.all_gather(payload, 'node', axis=0, tiled=True)]
    all_to_all x8 -> x1, starting transfers between devices: 60.9 us -> 4 us  [per_device(): lax.all_to_all(slots.reshape(inners, local, nodes, -1), 'inner', split_ax...]
    unnamed x4 -> x6, waiting for transfers between devices: 0.07 us -> 40.4 us
    all_to_all x0 -> x1, blocking collectives: none -> 12.6 us  [per_device(): lax.all_to_all(answer, 'inner', split_axis=0, concat_axis=0, tiled=True)]
    all_to_all x8 -> x0, local copies, waits for them, and re-layouts: 8.27 us -> none  [the longest x1 2.23 us: per_device(): lax.all_to_all(lax.all_to_all(send_grads.reshape(block_shape), 'node', sp...]
    reshape x8 -> x0, local copies, waits for them, and re-layouts: 6.18 us -> none  [the longest x2 2.32 us: per_device(): expert_out.reshape(block_shape)]
  transfers between devices with their start and end apart: 11 -> 6, of which waited for: 9 -> 6; matrix products, arithmetic and copies ran while one was open for 6% -> 2% of each run, Pallas kernels for 0% -> 0%
where the time goes in v1:
time: 482 us; the launch traced here: 481 us
  waiting for transfers between devices  416 us (86%)
  local copies, waits for them, and re-layouts  15.2 us (3%)
  matrix products  15.1 us (3%)
  between operations  14 us (3%)
  blocking collectives  12.6 us (3%)
    all_gather x1, waiting for transfers between devices, per_device(): gathered = lax.all_gather(payload, 'node', axis=0, tiled=True)  128 us
    reduce_scatter x1, waiting for transfers between devices, per_device(): total = lax.psum_scatter(partial, 'node', scatter_dimension=0, tiled=True)  117 us
    reduce_scatter x1, waiting for transfers between devices, per_device(): lax.psum_scatter(term_gate.astype(BF16), 'rep', scatter_dimension=1, tile...  68.2 us
    reduce_scatter x1, waiting for transfers between devices, per_device(): lax.psum_scatter(term_up.astype(BF16), 'rep', scatter_dimension=1, tiled=...  52.6 us
    unnamed x6, waiting for transfers between devices  40.4 us
    all_to_all x1, blocking collectives, per_device(): lax.all_to_all(answer, 'inner', split_axis=0, concat_axis=0, tiled=True)  12.6 us
    unnamed x21, local copies, waits for them, and re-layouts  10.4 us
    all_to_all x1, waiting for transfers between devices, per_device(): lax.all_to_all(slots.reshape(inners, local, nodes, -1), 'inner', split_ax...  10.1 us
  transfers between devices with their start and end apart: 6, of which 6 were waited for; matrix products, arithmetic and copies ran while one was open for 2% of the time, Pallas kernels for 0%

profile of v1, /device:TPU:7, one launch (start us, length us, event | category | flops | bytes accessed | tf_op | source)
XLA Modules:
  0.0 480.9 jit_solution(5165819835126251933)
XLA Ops:
  8.7 1.5 concatenate.17
  10.3 127.9 %all-gather.2.cloned.1.call-done = bf16[512,2176]{1,0:T(8,128)(2,1)} async-done(((bf16[16,2176]{1,0:T(8,128)(2,1)}), bf16[512,2176]{1,0:T(8,128)(2,1)}) %all-gather.2.cloned.1.call-update) | async-done | bytes 2228240 | tf_op jit(solution)/shard_map/all_gather | solution.py:32
  138.2 0.9 slice.44
  140.8 3.4 convolution_convert_fusion.1
  144.2 4.0 all-to-all-start
  148.2 10.1 %all-to-all-done = bf16[4,2,32,2176]{3,2,1,0:T(8,128)(2,1)S(1)} async-done(((bf16[4,2,32,2176]{3,2,1,0:T(8,128)(2,1)}), bf16[4,2,32,2176]{3,2,1,0:T(8,128)(2,1)S(1)}, u32[]{:S(2)}, u32[]{:S(2)}) %all-to-all-start) | async-done | bytes 1114144 | tf_op jit(solution)/shard_map/all_to_all | solution.py:41
  158.4 1.1 copy-done.2
  160.5 1.2 multiply_convert_fusion.1
  161.7 1.2 multiply_convert_fusion
  162.9 1.5 convolution_convert_fusion.2
  164.6 3.6 copy.69
  168.2 2.4 copy.72
  170.7 1.5 fusion.18
  173.4 12.6 %all_to_all.10 = bf16[4,2,32,2176]{3,2,1,0:T(8,128)(2,1)S(1)} all-to-all(bf16[4,2,32,2176]{3,2,1,0:T(8,128)(2,1)S(1)} %copy_bitcast_fusion), channel_id=1, replica_groups=mesh['node'=32,'inner'=4,'rep'=8] {'inner'}, dimensions={0} | all-to-all | bytes 2228224 | tf_op jit(solution)/shard_map/all_to_all | solution.py:70
  185.9 2.2 convolution_convert_fusion
  189.0 1.5 convolution_convert_fusion.4
  190.6 1.5 convolution_convert_fusion.3
  192.1 40.3 %reduce-scatter.13.cloned.1.call-done = bf16[128,512]{1,0:T(8,128)(2,1)} async-done(((bf16[1024,512]{1,0:T(8,128)(2,1)}), bf16[128,512]{1,0:T(8,128)(2,1)}) %reduce-scatter.13.cloned.1.call-update) | async-done | bytes 131088
  232.4 0.9 reshape.76
  234.1 116.8 %reduce-scatter.7.cloned.1.call-done = bf16[16,2176]{1,0:T(8,128)(2,1)} async-done(((bf16[512,2176]{1,0:T(8,128)(2,1)}), bf16[16,2176]{1,0:T(8,128)(2,1)}) %reduce-scatter.7.cloned.1.call-update) | async-done | bytes 69648 | tf_op jit(solution)/shard_map/reduce_scatter | solution.py:77
  350.9 1.3 slice_convert_fusion.1
  352.2 1.4 fusion.17
  353.6 68.2 %reduce-scatter.9.cloned.1.call-done = bf16[2,128,256]{2,1,0:T(8,128)(2,1)} async-done(((bf16[2,1024,256]{2,1,0:T(8,128)(2,1)}), bf16[2,128,256]{2,1,0:T(8,128)(2,1)}) %reduce-scatter.9.cloned.1.call-update) | async-done | bytes 131088 | tf_op jit(solution)/shard_map/reduce_scatter | solution.py:81
  421.8 52.6 %reduce-scatter.11.cloned.1.call-done = bf16[2,128,256]{2,1,0:T(8,128)(2,1)} async-done(((bf16[2,1024,256]{2,1,0:T(8,128)(2,1)}), bf16[2,128,256]{2,1,0:T(8,128)(2,1)}) %reduce-scatter.11.cloned.1.call-update) | async-done | bytes 131088 | tf_op jit(solution)/shard_map/reduce_scatter | solution.py:82
  (48 shorter events, 7.3 us)
Async XLA Ops:
  7.2 153.3 %copy-start = (bf16[2,256,1024]{2,1,0:T(8,128)(2,1)S(1)}, bf16[2,256,1024]{2,1,0:T(8,128)(2,1)}, u32[]{:S(2)}) copy-start(bf16[2,256,1024]{2,1,0:T(8,128)(2,1)} %param.13) | copy-start | bytes 3145732
  7.2 131.0 %all-gather.2.cloned.1.call-start = ((), (), s32[]{:S(2)}) async-start(), calls=%async_computation.6 | async-start | bytes 2297856 | tf_op jit(solution)/shard_map/all_gather | solution.py:32
  144.2 14.1 %all-to-all-start = ((bf16[4,2,32,2176]{3,2,1,0:T(8,128)(2,1)}), bf16[4,2,32,2176]{3,2,1,0:T(8,128)(2,1)S(1)}, u32[]{:S(2)}, u32[]{:S(2)}) async-start(bf16[4,2,32,2176]{3,2,1,0:T(8,128)(2,1)} %bitcast.1), calls=%async_computation | async-start | bytes 2228224 | tf_op jit(solution)/shard_map/all_to_all | solution.py:41
  148.2 84.1 %reduce-scatter.13.cloned.1.call-start = ((), (), s32[]{:S(2)}) async-start(), calls=%async_computation.10 | async-start | bytes 1179648
  158.3 1.2 copy-start.2
  158.4 1.5 copy-start.1
  170.7 180.2 %reduce-scatter.7.cloned.1.call-start = ((), (), s32[]{:S(2)}) async-start(), calls=%async_computation.7 | async-start | bytes 2297856 | tf_op jit(solution)/shard_map/reduce_scatter | solution.py:77
  170.7 1.5 copy-start.3
  170.7 1.5 copy-start.6
  172.2 1.0 copy-start.4
  188.1 0.9 copy-start.5
  188.1 2.5 copy-start.7
  188.1 233.7 %reduce-scatter.9.cloned.1.call-start = ((), (), s32[]{:S(2)}) async-start(), calls=%async_computation.8 | async-start | bytes 1179648 | tf_op jit(solution)/shard_map/reduce_scatter | solution.py:81
  190.5 283.8 %reduce-scatter.11.cloned.1.call-start = ((), (), s32[]{:S(2)}) async-start(), calls=%async_computation.9 | async-start | bytes 1179648 | tf_op jit(solution)/shard_map/reduce_scatter | solution.py:82
Sparse Core Ops, SparseCore 0:
  11.3 126.8 all-gather.1
  170.8 61.5 reduce-scatter.12
  235.8 115.0 reduce-scatter.6
  354.7 67.0 reduce-scatter.8
  425.6 48.7 reduce-scatter.10

commit v2 on v1

v2 whole, which is shorter than its diff:
```python
import functools

import jax
import jax.numpy as jnp
from jax import lax
from jax.experimental import pallas as pl
from jax.experimental.pallas import tpu as pltpu
from jax.sharding import PartitionSpec as P

BF16 = jnp.bfloat16
F32 = jnp.float32
LANES = 128
ROWS = 16
GROUP = 8
MESH = pl.DeviceIdType.MESH


def place(distance, nodes):
    if distance < nodes // 2:
        return GROUP * (distance // 4) + distance % 4
    back = nodes - 1 - distance
    return GROUP * (back // 4) + 4 + back % 4


def mm(a, b, contract):
    return lax.dot_general(a, b, ((contract[:1], contract[1:]), ((), ())), preferred_element_type=F32)


def kernel(
    sizes,
    tokens,
    out_grad,
    expert_ids,
    route_weight,
    gate_hbm,
    up_hbm,
    down_hbm,
    mixed,
    grad_tokens,
    grad_route,
    grad_gate,
    grad_up,
    grad_down,
    small,
    gathered,
    pick,
    slot_send,
    slot_got,
    answer_send,
    answer_got,
    partial,
    first,
    sums_left,
    sums_right,
    gate_w,
    up_w,
    down_w,
    terms,
    paired,
    crossed,
    weight_sem,
    ring_send,
    ring_recv,
    slot_send_sem,
    slot_recv_sem,
    answer_send_sem,
    answer_recv_sem,
    sum_send,
    sum_recv,
    pair_send,
    pair_recv,
    cross_send,
    cross_recv,
):
    nodes, inners, chips, width, ff, top, local = sizes
    chunks = nodes // GROUP
    half = nodes // 2
    total_lanes = 2 * width + LANES
    middle = (total_lanes // LANES + 1) // 2 * LANES
    halves = (pl.ds(0, middle), pl.ds(middle, total_lanes - middle))
    part = width // (2 * chips)
    node = lax.axis_index("node")
    inner = lax.axis_index("inner")
    rep = lax.axis_index("rep")
    chip = rep // 2
    core = lax.rem(rep, 2)
    right = {"node": lax.rem(node + 1, nodes)}
    left = {"node": lax.rem(node + nodes - 1, nodes)}
    partner = {"rep": rep + 1 - 2 * core}

    def inner_at(step):
        return {"inner": lax.rem(inner + step + inners, inners)}

    def chip_at(step):
        return {"rep": 2 * lax.rem(chip + step + chips, chips) + core}

    weight_copies = [
        pltpu.make_async_copy(src, dst, weight_sem.at[i])
        for i, (src, dst) in enumerate(((gate_hbm, gate_w), (up_hbm, up_w), (down_hbm, down_w)))
    ]
    for copy in weight_copies:
        copy.start()

    barrier = pltpu.get_barrier_semaphore()
    peers = (
        [right, left, partner]
        + [inner_at(d) for d in range(1, inners)]
        + [chip_at(d) for d in range(1, chips)]
    )
    for peer in peers:
        pl.semaphore_signal(barrier, inc=1, device_id=peer, device_id_type=MESH)

    small[...] = jnp.zeros_like(small)
    small[0, :, 0:top] = expert_ids[...].astype(F32)
    small[1, :, 0:top] = route_weight[...]
    weight = small[1]
    high = weight.astype(BF16).astype(F32)
    mid = (weight - high).astype(BF16).astype(F32)
    low = weight - high - mid
    meta = small[0] + pltpu.roll(high, 32, 1) + pltpu.roll(mid, 64, 1) + pltpu.roll(low, 96, 1)
    gathered[0:ROWS, 0:width] = tokens[...]
    gathered[0:ROWS, width : 2 * width] = out_grad[...]
    gathered[0:ROWS, 2 * width :] = meta.astype(BF16)

    pl.semaphore_wait(barrier, len(peers))
    pending = []

    def ring_copy(way, step, h):
        if way == 0:
            here, there, target = step, step + 1, right
        else:
            here, there, target = (nodes - step) % nodes, nodes - 1 - step, left
        return pltpu.make_async_remote_copy(
            src_ref=gathered.at[pl.ds(ROWS * place(here, nodes), ROWS), halves[h]],
            dst_ref=gathered.at[pl.ds(ROWS * place(there, nodes), ROWS), halves[h]],
            send_sem=ring_send.at[way, step, h],
            recv_sem=ring_recv.at[way, step, h],
            device_id=target,
            device_id_type=MESH,
        )

    steps = (half, half - 1)

    def ring_start(way, step, h):
        if step < steps[way]:
            copy = ring_copy(way, step, h)
            copy.start()
            pending.append(copy)

    def ring_wait(way, step, h):
        if step < steps[way]:
            ring_copy(way, step, h).wait_recv()

    per_chunk = inners * ROWS
    tokens_in = GROUP * ROWS

    def slot_copy(c, d):
        return pltpu.make_async_remote_copy(
            src_ref=slot_send.at[c, d],
            dst_ref=slot_got.at[c, d],
            send_sem=slot_send_sem.at[c, d],
            recv_sem=slot_recv_sem.at[c, d],
            device_id=inner_at(d),
            device_id_type=MESH,
        )

    def select(c):
        rows = pl.ds(tokens_in * c, tokens_in)
        ids = gathered[rows, 2 * width :].astype(F32).T[0:ROWS]
        top_row = lax.broadcasted_iota(jnp.int32, (ROWS, tokens_in), 0) < top
        owner = lax.broadcasted_iota(jnp.int32, (GROUP, tokens_in), 1) // ROWS
        same = owner == lax.broadcasted_iota(jnp.int32, (GROUP, tokens_in), 0)
        blocks = []
        for d in range(inners):
            for e in range(local):
                expert = (node * inners + lax.rem(inner + d, inners)) * local + e
                hit = jnp.where(jnp.logical_and(top_row, ids == expert.astype(F32)), 1.0, 0.0)
                hit = jnp.max(hit, axis=0, keepdims=True)
                blocks.append(jnp.where(same, jnp.broadcast_to(hit, same.shape), 0.0))
        onehot = jnp.concatenate(blocks, axis=0)
        pick[c] = onehot
        picked = mm(onehot.astype(BF16), gathered[rows, :], (1, 0)).astype(BF16)
        slot_got[c, 0] = picked[0:ROWS]
        for d in range(1, inners):
            slot_send[c, d] = picked[ROWS * d : ROWS * (d + 1)]
            copy = slot_copy(c, d)
            copy.start()
            pending.append(copy)

    for h in range(2):
        for way in range(2):
            ring_start(way, 0, h)
    for step in range(1, half + 1):
        for h in range(2):
            for way in range(2):
                ring_wait(way, step - 1, h)
                ring_start(way, step, h)
        if step % 4 == 0:
            select(step // 4 - 1)

    for copy in weight_copies:
        copy.wait()
    for c in range(chunks):
        for d in range(1, inners):
            slot_copy(c, d).wait_recv()

    count = nodes * inners
    blocks = chunks * inners
    lane = lax.broadcasted_iota(jnp.int32, (count, LANES), 1) < top

    def of_expert(lanes, e):
        rows = slot_got[:, :, :, lanes].astype(F32)
        return rows.reshape(blocks, local, GROUP, rows.shape[-1])[:, e].reshape(count, rows.shape[-1])

    results = []
    for e in range(local):
        rows = of_expert(slice(0, width), e).astype(BF16)
        cotangent = of_expert(slice(width, 2 * width), e)
        extra = of_expert(slice(2 * width, total_lanes), e)
        expert = (node * inners + inner) * local + e
        mine = jnp.logical_and(lane, extra == expert.astype(F32))
        weights = pltpu.roll(extra, 96, 1) + pltpu.roll(extra, 64, 1) + pltpu.roll(extra, 32, 1)
        weight = jnp.sum(jnp.where(mine, weights, 0.0), axis=1, keepdims=True)
        scaled = (weight * cotangent).astype(BF16)
        gate_pre = mm(rows, gate_w[e], (1, 0))
        up_pre = mm(rows, up_w[e], (1, 0))
        act_grad = mm(scaled, down_w[e], (1, 1))
        gate_sig = jax.nn.sigmoid(gate_pre)
        silu = gate_pre * gate_sig
        activation = (silu * up_pre).astype(BF16)
        up_grad = (act_grad * silu).astype(BF16)
        gate_grad = (act_grad * up_pre * (gate_sig * (1.0 + gate_pre * (1.0 - gate_sig)))).astype(BF16)
        expert_out = mm(activation, down_w[e], (1, 0))
        back = mm(gate_grad, gate_w[e], (1, 1)) + mm(up_grad, up_w[e], (1, 1))
        route = jnp.sum(cotangent * expert_out, axis=1, keepdims=True)
        route = jnp.where(mine, jnp.broadcast_to(route, mine.shape), 0.0)
        results.append((weight * expert_out, back, route, rows, scaled, activation, up_grad, gate_grad))

    for i, lanes in enumerate((slice(0, width), slice(width, 2 * width), slice(2 * width, total_lanes))):
        both = [results[e][i].reshape(blocks, 1, GROUP, -1) for e in range(local)]
        both = jnp.concatenate(both, axis=1).reshape(chunks, inners, ROWS, -1).astype(BF16)
        answer_send[:, :, :, lanes] = both
        answer_got[:, 0, :, lanes] = both[:, 0]

    def answer_copy(c, d):
        return pltpu.make_async_remote_copy(
            src_ref=answer_send.at[c, d],
            dst_ref=answer_got.at[c, d],
            send_sem=answer_send_sem.at[c, d],
            recv_sem=answer_recv_sem.at[c, d],
            device_id=inner_at(-d),
            device_id_type=MESH,
        )

    for c in reversed(range(chunks)):
        for d in range(1, inners):
            copy = answer_copy(c, d)
            copy.start()
            pending.append(copy)

    for e in range(local):
        _, _, _, rows, scaled, activation, up_grad, gate_grad = results[e]
        for i, grad in enumerate((gate_grad, up_grad)):
            term = mm(rows, grad, (0, 0)).astype(BF16)
            for r in range(2 * chips):
                at = (i * local + e) * part
                terms[r % 2, r // 2, at : at + part, :] = term[r * part : (r + 1) * part]
        term = mm(activation, scaled, (0, 0)).astype(BF16)
        for r in range(2 * chips):
            at = 2 * local * part
            terms[r % 2, r // 2, at : at + ff, e * part : (e + 1) * part] = term[:, r * part : (r + 1) * part]

    def pair_copy(d):
        return pltpu.make_async_remote_copy(
            src_ref=terms.at[1 - core, lax.rem(chip + d, chips)],
            dst_ref=paired.at[d],
            send_sem=pair_send.at[d],
            recv_sem=pair_recv.at[d],
            device_id=partner,
            device_id_type=MESH,
        )

    def cross_copy(d):
        return pltpu.make_async_remote_copy(
            src_ref=paired.at[d],
            dst_ref=crossed.at[d - 1],
            send_sem=cross_send.at[d - 1],
            recv_sem=cross_recv.at[d - 1],
            device_id=chip_at(d),
            device_id_type=MESH,
        )

    order = sorted(range(chips), key=lambda d: -min(d, chips - d))
    for d in order:
        copy = pair_copy(d)
        copy.start()
        pending.append(copy)

    def pair_add(d):
        pair_copy(d).wait_recv()
        own = terms[core, lax.rem(chip + d, chips)]
        paired[d] = (paired[d].astype(F32) + own.astype(F32)).astype(BF16)
        if d > 0:
            copy = cross_copy(d)
            copy.start()
            pending.append(copy)

    def combine(c):
        for d in range(1, inners):
            answer_copy(c, d).wait_recv()
        answers = answer_got[c].reshape(per_chunk, total_lanes)
        partial[pl.ds(tokens_in * c, tokens_in), :] = mm(pick[c].astype(BF16), answers, (0, 0))

    def partial_of(distance, h):
        return partial[pl.ds(ROWS * place(distance % nodes, nodes), ROWS), halves[h]]

    landed = (sums_left, sums_right)

    def sum_copy(way, step, h):
        source = first.at[way] if step == 0 else landed[way].at[step - 1]
        return pltpu.make_async_remote_copy(
            src_ref=source.at[:, halves[h]],
            dst_ref=landed[way].at[step, :, halves[h]],
            send_sem=sum_send.at[way, step, h],
            recv_sem=sum_recv.at[way, step, h],
            device_id=(left, right)[way],
            device_id_type=MESH,
        )

    def sum_step(way, step, h):
        distance = half - step if way == 0 else half + 1 + step
        mine = partial_of(distance, h)
        if step == 0:
            first[way, :, halves[h]] = mine.astype(BF16)
        else:
            sum_copy(way, step - 1, h).wait_recv()
            got = landed[way][step - 1, :, halves[h]]
            landed[way][step - 1, :, halves[h]] = (got.astype(F32) + mine).astype(BF16)
        copy = sum_copy(way, step, h)
        copy.start()
        pending.append(copy)

    combine(chunks - 1)
    beside = {}
    for k in range(1, chunks):
        beside.setdefault(4 * k - 3, []).append(functools.partial(combine, chunks - 1 - k))
    for k, d in enumerate(order):
        beside.setdefault(min(2 + k, half - 2), []).append(functools.partial(pair_add, d))
    for step in range(half):
        for h in range(2):
            for way in range(2):
                if step < steps[way]:
                    sum_step(way, step, h)
        for work in beside.get(step, ()):
            work()

    at = 0
    summed = paired[0].astype(F32)
    for d in range(1, chips):
        cross_copy(d).wait_recv()
        summed = summed + crossed[d - 1].astype(F32)
    summed = summed.astype(BF16)
    for i, out in enumerate((grad_gate, grad_up)):
        for e in range(local):
            at = (i * local + e) * part
            out[e] = summed[at : at + part]
    at = 2 * local * part
    for e in range(local):
        grad_down[e] = summed[at : at + ff, e * part : (e + 1) * part]

    for h in range(2):
        for way in range(2):
            sum_copy(way, steps[way] - 1, h).wait_recv()
    total = partial[0:ROWS, :] + sums_left[half - 1].astype(F32) + sums_right[half - 2].astype(F32)
    mixed[...] = total[:, 0:width].astype(BF16)
    grad_tokens[...] = total[:, width : 2 * width].astype(BF16)
    grad_route[...] = total[:, 2 * width :][:, 0:top]

    for copy in pending:
        copy.wait_send()


def per_device(tokens, out_grad, expert_ids, route_weight, gate_weight, up_weight, down_weight):
    width = tokens.shape[1]
    top = expert_ids.shape[1]
    local, _, ff = gate_weight.shape
    nodes = lax.axis_size("node")
    inners = lax.axis_size("inner")
    reps = lax.axis_size("rep")
    chips = reps // 2
    part = width // reps
    lanes = 2 * width + LANES
    chunks = nodes // GROUP
    half = nodes // 2
    slice_shape = (2 * local * part + ff, ff)
    count = nodes * ROWS
    vmem = pl.BlockSpec(memory_space=pltpu.VMEM)
    anywhere = pl.BlockSpec(memory_space=pl.ANY)
    dma = pltpu.SemaphoreType.DMA
    others = max(1, chips - 1)
    return pl.pallas_call(
        functools.partial(kernel, (nodes, inners, chips, width, ff, top, local)),
        out_shape=(
            jax.ShapeDtypeStruct((ROWS, width), BF16),
            jax.ShapeDtypeStruct((ROWS, width), BF16),
            jax.ShapeDtypeStruct((ROWS, top), F32),
            jax.ShapeDtypeStruct((local, part, ff), BF16),
            jax.ShapeDtypeStruct((local, part, ff), BF16),
            jax.ShapeDtypeStruct((local, ff, part), BF16),
        ),
        in_specs=[vmem] * 4 + [anywhere] * 3,
        out_specs=[vmem] * 6,
        scratch_shapes=[
            pltpu.VMEM((2, ROWS, LANES), F32),
            pltpu.VMEM((count, lanes), BF16),
            pltpu.VMEM((chunks, inners * ROWS, GROUP * ROWS), F32),
            pltpu.VMEM((chunks, inners, ROWS, lanes), BF16),
            pltpu.VMEM((chunks, inners, ROWS, lanes), BF16),
            pltpu.VMEM((chunks, inners, ROWS, lanes), BF16),
            pltpu.VMEM((chunks, inners, ROWS, lanes), BF16),
            pltpu.VMEM((count, lanes), F32),
            pltpu.VMEM((2, ROWS, lanes), BF16),
            pltpu.VMEM((half, ROWS, lanes), BF16),
            pltpu.VMEM((half - 1, ROWS, lanes), BF16),
            pltpu.VMEM(gate_weight.shape, BF16),
            pltpu.VMEM(up_weight.shape, BF16),
            pltpu.VMEM(down_weight.shape, BF16),
            pltpu.VMEM((2, chips) + slice_shape, BF16),
            pltpu.VMEM((chips,) + slice_shape, BF16),
            pltpu.VMEM((others,) + slice_shape, BF16),
            dma((3,)),
            dma((2, half, 2)),
            dma((2, half, 2)),
            dma((chunks, inners)),
            dma((chunks, inners)),
            dma((chunks, inners)),
            dma((chunks, inners)),
            dma((2, half, 2)),
            dma((2, half, 2)),
            dma((chips,)),
            dma((chips,)),
            dma((others,)),
            dma((others,)),
        ],
        compiler_params=pltpu.CompilerParams(
            collective_id=0, has_side_effects=True, vmem_limit_bytes=56 * 1024 * 1024
        ),
        cost_estimate=pl.CostEstimate(
            flops=2 * 9 * local * count // ROWS * inners * width * ff,
            bytes_accessed=12 * local * width * ff,
            transcendentals=local * count * ff,
        ),
    )(tokens, out_grad, expert_ids, route_weight, gate_weight, up_weight, down_weight)


def solution(mesh):
    split = P(("node", "inner", "rep"), None)
    held = P(("node", "inner"), None, None)
    return jax.shard_map(
        per_device,
        mesh=mesh,
        in_specs=(split,) * 4 + (held,) * 3,
        out_specs=(split,) * 3
        + (P(("node", "inner"), "rep", None),) * 2
        + (P(("node", "inner"), None, "rep"),),
        check_vma=False,
    )
```

time: 482 us -> 149 us (0.31)
  the two profiles are of different devices: /device:TPU:7 before, /device:TPU:2 now
where the time goes in v2:
time: 149 us
  Pallas kernels  142 us (95%)
  local copies, waits for them, and re-layouts  5.96 us (4%)
    pallas_call x1, Pallas kernels, per_device(): pl.pallas_call(functools.partial(kernel, (nodes, inners, chips, width, ff...  142 us
    unnamed x14, local copies, waits for them, and re-layouts  5.96 us

profile of v2, /device:TPU:2, one launch (start us, length us, event | category | flops | bytes accessed | tf_op | source)
XLA Modules:
  0.0 149.0 jit_solution(12366883268087117455)
XLA Ops:
  0.6 142.3 %shard_map.118 = (bf16[16,1024]{1,0:T(8,128)(2,1)}, bf16[16,1024]{1,0:T(8,128)(2,1)}, f32[16,10]{1,0:T(8,128)}, bf16[2,128,256]{2,1,0:T(8,128)(2,1)}, bf16[2,128...) custom-call(bf16[16,1024]{1,0:T(8,128)(2,1)} %tokens.1, bf16[16,1024]{1,0:T(8,128)(2,1)} %out_grad.1, ...), custom_call_target="tpu_custom_call" | custom-call | flops 1207959552 | bytes 6291456 | tf_op jit(solution)/shard_map/pallas_call | solution.py:401
  143.0 0.0 copy-start.2
  143.0 1.4 copy.19
  144.4 0.0 copy-start.3
  144.4 1.4 copy.20
  145.8 0.0 copy-done.3
  145.8 0.6 copy.21
  146.4 0.0 copy-done.2
  146.4 0.0 copy-start.1
  146.4 0.7 copy.22
  147.1 0.3 copy-done.1
  147.3 0.0 copy-start
  147.4 0.7 copy.23
  148.0 0.3 copy-done
  148.3 0.7 copy.24
Async XLA Ops:
  143.0 3.4 %copy-start.2 = (bf16[2,128,256]{2,1,0:T(8,128)(2,1)S(1)}, bf16[2,128,256]{2,1,0:T(8,128)(2,1)}, u32[]{:S(2)}) copy-start(bf16[2,128,256]{2,1,0:T(8,128)(2,1)} %get-tuple-element.15) | copy-start | bytes 393220
  144.4 1.4 copy-start.3
  146.4 1.0 copy-start.1
  147.3 1.0 copy-start

commit v3 on v2

--- a/solution.py
+++ b/solution.py
@@ -13,6 +13,11 @@
 ROWS = 16
 GROUP = 8
 MESH = pl.DeviceIdType.MESH
+OUT_STRIDE = 3
+BACK_STRIDE = 3
+ADD_FROM = 4
+ADD_EVERY = 2
+SPLIT = 2
 
 
 def place(distance, nodes):
@@ -20,6 +25,22 @@
         return GROUP * (distance // 4) + distance % 4
     back = nodes - 1 - distance
     return GROUP * (back // 4) + 4 + back % 4
+
+
+def parent_of(distance, stride):
+    return distance - stride if distance % stride == 0 else distance - 1
+
+
+def tree_order(half, stride):
+    when = {0: 0.0}
+    after = {distance: [] for distance in range(half + 1)}
+    for distance in range(1, half + 1):
+        parent = parent_of(distance, stride)
+        after[parent].insert(0, distance)
+        when[distance] = when[parent] + 2.6 + 0.65 * (distance - parent)
+    for followers in after.values():
+        followers.sort(reverse=True)
+    return sorted(when, key=lambda distance: when[distance]), after
 
 
 def mm(a, b, contract):
@@ -49,9 +70,8 @@
     answer_send,
     answer_got,
     partial,
-    first,
-    sums_left,
-    sums_right,
+    sums_out,
+    sums_in,
     gate_w,
     up_w,
     down_w,
@@ -84,9 +104,10 @@
     rep = lax.axis_index("rep")
     chip = rep // 2
     core = lax.rem(rep, 2)
-    right = {"node": lax.rem(node + 1, nodes)}
-    left = {"node": lax.rem(node + nodes - 1, nodes)}
     partner = {"rep": rep + 1 - 2 * core}
+
+    def node_at(step):
+        return {"node": lax.rem(node + step + nodes, nodes)}
 
     def inner_at(step):
         return {"inner": lax.rem(inner + step + inners, inners)}
@@ -103,7 +124,8 @@
 
     barrier = pltpu.get_barrier_semaphore()
     peers = (
-        [right, left, partner]
+        [node_at(way * step) for step in sorted({1, OUT_STRIDE, BACK_STRIDE}) for way in (1, -1)]
+        + [partner]
         + [inner_at(d) for d in range(1, inners)]
         + [chip_at(d) for d in range(1, chips)]
     )
@@ -125,31 +147,27 @@
     pl.semaphore_wait(barrier, len(peers))
     pending = []
 
-    def ring_copy(way, step, h):
-        if way == 0:
-            here, there, target = step, step + 1, right
-        else:
-            here, there, target = (nodes - step) % nodes, nodes - 1 - step, left
+    order, after = tree_order(half, OUT_STRIDE)
+    back_order, back_after = tree_order(half, BACK_STRIDE)
+    back_order = [distance for distance in reversed(back_order) if distance > 0]
+    reach = (half, half - 1)
+
+    def at(way, distance):
+        return place(distance if way == 0 else (nodes - distance) % nodes, nodes)
+
+    def block(way, distance):
+        return pl.ds(ROWS * at(way, distance), ROWS)
+
+    def gather_copy(way, distance, h):
+        parent = parent_of(distance, OUT_STRIDE)
         return pltpu.make_async_remote_copy(
-            src_ref=gathered.at[pl.ds(ROWS * place(here, nodes), ROWS), halves[h]],
-            dst_ref=gathered.at[pl.ds(ROWS * place(there, nodes), ROWS), halves[h]],
-            send_sem=ring_send.at[way, step, h],
-            recv_sem=ring_recv.at[way, step, h],
-            device_id=target,
+            src_ref=gathered.at[block(way, parent), halves[h]],
+            dst_ref=gathered.at[block(way, distance), halves[h]],
+            send_sem=ring_send.at[way, distance - 1, h],
+            recv_sem=ring_recv.at[way, distance - 1, h],
+            device_id=node_at((distance - parent) * (1, -1)[way]),
             device_id_type=MESH,
         )
-
-    steps = (half, half - 1)
-
-    def ring_start(way, step, h):
-        if step < steps[way]:
-            copy = ring_copy(way, step, h)
-            copy.start()
-            pending.append(copy)
-
-    def ring_wait(way, step, h):
-        if step < steps[way]:
-            ring_copy(way, step, h).wait_recv()
 
     per_chunk = inners * ROWS
     tokens_in = GROUP * ROWS
@@ -187,60 +205,51 @@
             copy.start()
             pending.append(copy)
 
-    for h in range(2):
-        for way in range(2):
-            ring_start(way, 0, h)
-    for step in range(1, half + 1):
-        for h in range(2):
-            for way in range(2):
-                ring_wait(way, step - 1, h)
-                ring_start(way, step, h)
-        if step % 4 == 0:
-            select(step // 4 - 1)
-
-    for copy in weight_copies:
-        copy.wait()
-    for c in range(chunks):
-        for d in range(1, inners):
-            slot_copy(c, d).wait_recv()
-
-    count = nodes * inners
-    blocks = chunks * inners
-    lane = lax.broadcasted_iota(jnp.int32, (count, LANES), 1) < top
-
-    def of_expert(lanes, e):
-        rows = slot_got[:, :, :, lanes].astype(F32)
-        return rows.reshape(blocks, local, GROUP, rows.shape[-1])[:, e].reshape(count, rows.shape[-1])
-
-    results = []
-    for e in range(local):
-        rows = of_expert(slice(0, width), e).astype(BF16)
-        cotangent = of_expert(slice(width, 2 * width), e)
-        extra = of_expert(slice(2 * width, total_lanes), e)
-        expert = (node * inners + inner) * local + e
-        mine = jnp.logical_and(lane, extra == expert.astype(F32))
-        weights = pltpu.roll(extra, 96, 1) + pltpu.roll(extra, 64, 1) + pltpu.roll(extra, 32, 1)
-        weight = jnp.sum(jnp.where(mine, weights, 0.0), axis=1, keepdims=True)
-        scaled = (weight * cotangent).astype(BF16)
-        gate_pre = mm(rows, gate_w[e], (1, 0))
-        up_pre = mm(rows, up_w[e], (1, 0))
-        act_grad = mm(scaled, down_w[e], (1, 1))
-        gate_sig = jax.nn.sigmoid(gate_pre)
-        silu = gate_pre * gate_sig
-        activation = (silu * up_pre).astype(BF16)
-        up_grad = (act_grad * silu).astype(BF16)
-        gate_grad = (act_grad * up_pre * (gate_sig * (1.0 + gate_pre * (1.0 - gate_sig)))).astype(BF16)
-        expert_out = mm(activation, down_w[e], (1, 0))
-        back = mm(gate_grad, gate_w[e], (1, 1)) + mm(up_grad, up_w[e], (1, 1))
-        route = jnp.sum(cotangent * expert_out, axis=1, keepdims=True)
-        route = jnp.where(mine, jnp.broadcast_to(route, mine.shape), 0.0)
-        results.append((weight * expert_out, back, route, rows, scaled, activation, up_grad, gate_grad))
-
-    for i, lanes in enumerate((slice(0, width), slice(width, 2 * width), slice(2 * width, total_lanes))):
-        both = [results[e][i].reshape(blocks, 1, GROUP, -1) for e in range(local)]
-        both = jnp.concatenate(both, axis=1).reshape(chunks, inners, ROWS, -1).astype(BF16)
-        answer_send[:, :, :, lanes] = both
-        answer_got[:, 0, :, lanes] = both[:, 0]
+    batches = [range(0, chunks // 2), range(chunks // 2, chunks)]
+    if SPLIT == 3 and chunks == 4:
+        batches = [range(0, 2), range(2, 3), range(3, 4)]
+    kept = [[] for _ in range(local)]
+
+    def of_expert(batch, lanes, e):
+        rows = slot_got[batch.start : batch.stop, :, :, lanes].astype(F32)
+        rows = rows.reshape(len(batch) * inners, local, GROUP, rows.shape[-1])[:, e]
+        return rows.reshape(len(batch) * inners * GROUP, rows.shape[-1])
+
+    def experts(batch):
+        results = []
+        for e in range(local):
+            rows = of_expert(batch, slice(0, width), e).astype(BF16)
+            cotangent = of_expert(batch, slice(width, 2 * width), e)
+            extra = of_expert(batch, slice(2 * width, total_lanes), e)
+            lane = lax.broadcasted_iota(jnp.int32, extra.shape, 1) < top
+            expert = (node * inners + inner) * local + e
+            mine = jnp.logical_and(lane, extra == expert.astype(F32))
+            weights = pltpu.roll(extra, 96, 1) + pltpu.roll(extra, 64, 1) + pltpu.roll(extra, 32, 1)
+            weight = jnp.sum(jnp.where(mine, weights, 0.0), axis=1, keepdims=True)
+            scaled = (weight * cotangent).astype(BF16)
+            gate_pre = mm(rows, gate_w[e], (1, 0))
+            up_pre = mm(rows, up_w[e], (1, 0))
+            yield
+            act_grad = mm(scaled, down_w[e], (1, 1))
+            gate_sig = jax.nn.sigmoid(gate_pre)
+            silu = gate_pre * gate_sig
+            activation = (silu * up_pre).astype(BF16)
+            up_grad = (act_grad * silu).astype(BF16)
+            gate_grad = act_grad * up_pre * (gate_sig * (1.0 + gate_pre * (1.0 - gate_sig)))
+            gate_grad = gate_grad.astype(BF16)
+            yield
+            expert_out = mm(activation, down_w[e], (1, 0))
+            back = mm(gate_grad, gate_w[e], (1, 1)) + mm(up_grad, up_w[e], (1, 1))
+            route = jnp.sum(cotangent * expert_out, axis=1, keepdims=True)
+            route = jnp.where(mine, jnp.broadcast_to(route, mine.shape), 0.0)
+            results.append((weight * expert_out, back, route))
+            kept[e].append((rows, scaled, activation, up_grad, gate_grad))
+            yield
+        for i, lanes in enumerate((slice(0, width), slice(width, 2 * width), slice(2 * width, total_lanes))):
+            both = [results[e][i].reshape(len(batch) * inners, 1, GROUP, -1) for e in range(local)]
+            both = jnp.concatenate(both, axis=1).reshape(len(batch), inners, ROWS, -1).astype(BF16)
+            answer_send[batch.start : batch.stop, :, :, lanes] = both
+            answer_got[batch.start : batch.stop, 0, :, lanes] = both[:, 0]
 
     def answer_copy(c, d):
         return pltpu.make_async_remote_copy(
@@ -252,23 +261,68 @@
             device_id_type=MESH,
         )
 
-    for c in reversed(range(chunks)):
-        for d in range(1, inners):
-            copy = answer_copy(c, d)
-            copy.start()
-            pending.append(copy)
+    def serve(batch):
+        for c in batch:
+            for d in range(1, inners):
+                slot_copy(c, d).wait_recv()
+        yield from experts(batch)
+        for c in reversed(batch):
+            for d in range(1, inners):
+                copy = answer_copy(c, d)
+                copy.start()
+                pending.append(copy)
+
+    early = serve(batches[0])
+    rest = None
+    seen = set()
+    for distance in order:
+        for h in range(2):
+            for way in range(2):
+                if distance > reach[way]:
+                    continue
+                if distance > 0:
+                    gather_copy(way, distance, h).wait_recv()
+                for follower in after[distance]:
+                    if follower <= reach[way]:
+                        copy = gather_copy(way, follower, h)
+                        copy.start()
+                        pending.append(copy)
+        before = set(seen)
+        seen.update(at(way, distance) for way in range(2) if distance <= reach[way])
+        if rest is not None:
+            rest += 1
+            if rest == 2:
+                for copy in weight_copies:
+                    copy.wait()
+            if rest >= 2:
+                next(early, None)
+        for c in range(chunks):
+            wanted = set(range(GROUP * c, GROUP * (c + 1)))
+            if wanted <= seen and not wanted <= before:
+                select(c)
+                if c == batches[0][-1]:
+                    rest = 0
+
+    for batch in batches[1:]:
+        for _ in early:
+            pass
+        early = serve(batch)
+    for _ in early:
+        pass
 
     for e in range(local):
-        _, _, _, rows, scaled, activation, up_grad, gate_grad = results[e]
+        rows, scaled, activation, up_grad, gate_grad = (
+            jnp.concatenate(pair, axis=0) for pair in zip(*kept[e])
+        )
         for i, grad in enumerate((gate_grad, up_grad)):
             term = mm(rows, grad, (0, 0)).astype(BF16)
             for r in range(2 * chips):
-                at = (i * local + e) * part
-                terms[r % 2, r // 2, at : at + part, :] = term[r * part : (r + 1) * part]
+                low = (i * local + e) * part
+                terms[r % 2, r // 2, low : low + part, :] = term[r * part : (r + 1) * part]
         term = mm(activation, scaled, (0, 0)).astype(BF16)
         for r in range(2 * chips):
-            at = 2 * local * part
-            terms[r % 2, r // 2, at : at + ff, e * part : (e + 1) * part] = term[:, r * part : (r + 1) * part]
+            low = 2 * local * part
+            terms[r % 2, r // 2, low : low + ff, e * part : (e + 1) * part] = term[:, r * part : (r + 1) * part]
 
     def pair_copy(d):
         return pltpu.make_async_remote_copy(
@@ -290,8 +344,8 @@
             device_id_type=MESH,
         )
 
-    order = sorted(range(chips), key=lambda d: -min(d, chips - d))
-    for d in order:
+    chip_order = sorted(range(chips), key=lambda d: -min(d, chips - d))
+    for d in chip_order:
         copy = pair_copy(d)
         copy.start()
         pending.append(copy)
@@ -311,50 +365,62 @@
         answers = answer_got[c].reshape(per_chunk, total_lanes)
         partial[pl.ds(tokens_in * c, tokens_in), :] = mm(pick[c].astype(BF16), answers, (0, 0))
 
-    def partial_of(distance, h):
-        return partial[pl.ds(ROWS * place(distance % nodes, nodes), ROWS), halves[h]]
-
-    landed = (sums_left, sums_right)
-
-    def sum_copy(way, step, h):
-        source = first.at[way] if step == 0 else landed[way].at[step - 1]
+    def sum_copy(way, distance, h):
+        parent = parent_of(distance, BACK_STRIDE)
         return pltpu.make_async_remote_copy(
-            src_ref=source.at[:, halves[h]],
-            dst_ref=landed[way].at[step, :, halves[h]],
-            send_sem=sum_send.at[way, step, h],
-            recv_sem=sum_recv.at[way, step, h],
-            device_id=(left, right)[way],
+            src_ref=sums_out.at[way, distance - 1, :, halves[h]],
+            dst_ref=sums_in.at[way, distance - 1, :, halves[h]],
+            send_sem=sum_send.at[way, distance - 1, h],
+            recv_sem=sum_recv.at[way, distance - 1, h],
+            device_id=node_at((distance - parent) * (-1, 1)[way]),
             device_id_type=MESH,
         )
 
-    def sum_step(way, step, h):
-        distance = half - step if way == 0 else half + 1 + step
-        mine = partial_of(distance, h)
-        if step == 0:
-            first[way, :, halves[h]] = mine.astype(BF16)
-        else:
-            sum_copy(way, step - 1, h).wait_recv()
-            got = landed[way][step - 1, :, halves[h]]
-            landed[way][step - 1, :, halves[h]] = (got.astype(F32) + mine).astype(BF16)
-        copy = sum_copy(way, step, h)
-        copy.start()
-        pending.append(copy)
-
-    combine(chunks - 1)
-    beside = {}
-    for k in range(1, chunks):
-        beside.setdefault(4 * k - 3, []).append(functools.partial(combine, chunks - 1 - k))
-    for k, d in enumerate(order):
-        beside.setdefault(min(2 + k, half - 2), []).append(functools.partial(pair_add, d))
-    for step in range(half):
+    def arrived(way, distance, h):
+        total = None
+        for follower in back_after[distance]:
+            if follower <= reach[way]:
+                sum_copy(way, follower, h).wait_recv()
+                got = sums_in[way, follower - 1, :, halves[h]].astype(F32)
+                total = got if total is None else total + got
+        return total
+
+    combined = set()
+
+    def combine_for(distance):
+        for way in range(2):
+            if 0 <= distance <= reach[way]:
+                c = at(way, distance) // GROUP
+                if c not in combined:
+                    combined.add(c)
+                    combine(c)
+
+    add_every = ADD_EVERY if (chips - 1) * ADD_EVERY + ADD_FROM < half else 1
+    first_add = ADD_FROM if add_every > 1 else 0
+    combine_for(back_order[0])
+    for step, distance in enumerate(back_order):
+        combine_for(distance)
         for h in range(2):
             for way in range(2):
-                if step < steps[way]:
-                    sum_step(way, step, h)
-        for work in beside.get(step, ()):
-            work()
-
-    at = 0
+                if distance > reach[way]:
+                    continue
+                total = partial[block(way, distance), halves[h]]
+                got = arrived(way, distance, h)
+                if got is not None:
+                    total = total + got
+                sums_out[way, distance - 1, :, halves[h]] = total.astype(BF16)
+                copy = sum_copy(way, distance, h)
+                copy.start()
+                pending.append(copy)
+        for ahead in back_order[step + 1 : step + 3]:
+            combine_for(ahead)
+        turn, off = divmod(step - first_add, add_every)
+        if off == 0 and 0 <= turn < chips:
+            pair_add(chip_order[turn])
+    for c in range(chunks):
+        if c not in combined:
+            combine(c)
+
     summed = paired[0].astype(F32)
     for d in range(1, chips):
         cross_copy(d).wait_recv()
@@ -362,22 +428,36 @@
     summed = summed.astype(BF16)
     for i, out in enumerate((grad_gate, grad_up)):
         for e in range(local):
-            at = (i * local + e) * part
-            out[e] = summed[at : at + part]
-    at = 2 * local * part
+            low = (i * local + e) * part
+            out[e] = summed[low : low + part]
+    low = 2 * local * part
     for e in range(local):
-        grad_down[e] = summed[at : at + ff, e * part : (e + 1) * part]
-
-    for h in range(2):
-        for way in range(2):
-            sum_copy(way, steps[way] - 1, h).wait_recv()
-    total = partial[0:ROWS, :] + sums_left[half - 1].astype(F32) + sums_right[half - 2].astype(F32)
-    mixed[...] = total[:, 0:width].astype(BF16)
-    grad_tokens[...] = total[:, width : 2 * width].astype(BF16)
-    grad_route[...] = total[:, 2 * width :][:, 0:top]
+        grad_down[e] = summed[low : low + ff, e * part : (e + 1) * part]
+
+    for h, low in ((0, 0), (1, middle)):
+        total = partial[0:ROWS, halves[h]] + arrived(0, 0, h) + arrived(1, 0, h)
+        for out, begin, size in ((mixed, 0, width), (grad_tokens, width, width), (grad_route, 2 * width, LANES)):
+            start, stop = max(begin, low), min(begin + size, low + total.shape[1])
+            if start < stop:
+                value = total[:, start - low : stop - low]
+                if size == LANES:
+                    out[...] = value[:, 0:top]
+                else:
+                    out[:, start - begin : stop - begin] = value.astype(BF16)
 
     for copy in pending:
         copy.wait_send()
+
+
+def copy_out(*refs):
+    count = (len(refs) - 1) // 2
+    copies = [
+        pltpu.make_async_copy(refs[i], refs[count + i], refs[-1].at[i]) for i in range(count)
+    ]
+    for copy in copies:
+        copy.start()
+    for copy in copies:
+        copy.wait()
 
 
 def per_device(tokens, out_grad, expert_ids, route_weight, gate_weight, up_weight, down_weight):
@@ -398,7 +478,7 @@
     anywhere = pl.BlockSpec(memory_space=pl.ANY)
     dma = pltpu.SemaphoreType.DMA
     others = max(1, chips - 1)
-    return pl.pallas_call(
+    results = pl.pallas_call(
         functools.partial(kernel, (nodes, inners, chips, width, ff, top, local)),
         out_shape=(
             jax.ShapeDtypeStruct((ROWS, width), BF16),
@@ -419,9 +499,8 @@
             pltpu.VMEM((chunks, inners, ROWS, lanes), BF16),
             pltpu.VMEM((chunks, inners, ROWS, lanes), BF16),
             pltpu.VMEM((count, lanes), F32),
-            pltpu.VMEM((2, ROWS, lanes), BF16),
-            pltpu.VMEM((half, ROWS, lanes), BF16),
-            pltpu.VMEM((half - 1, ROWS, lanes), BF16),
+            pltpu.VMEM((2, half, ROWS, lanes), BF16),
+            pltpu.VMEM((2, half, ROWS, lanes), BF16),
             pltpu.VMEM(gate_weight.shape, BF16),
             pltpu.VMEM(up_weight.shape, BF16),
             pltpu.VMEM(down_weight.shape, BF16),
@@ -451,6 +530,13 @@
             transcendentals=local * count * ff,
         ),
     )(tokens, out_grad, expert_ids, route_weight, gate_weight, up_weight, down_weight)
+    return pl.pallas_call(
+        copy_out,
+        out_shape=[jax.ShapeDtypeStruct(result.shape, result.dtype) for result in results],
+        in_specs=[anywhere] * len(results),
+        out_specs=[anywhere] * len(results),
+        scratch_shapes=[dma((len(results),))],
+    )(*results)
 
 
 def solution(mesh):

time: 149 us -> 141 us (0.946)
  local copies, waits for them, and re-layouts: 5.96 us -> 0 us
  Pallas kernels: 142 us -> 140 us
    pallas_call x1, Pallas kernels: 142 us -> 124 us  [per_device(): pl.pallas_call(functools.partial(kernel, (nodes, inners, chips, width, ff...]
    pallas_call x0 -> x1, Pallas kernels: none -> 15.3 us  [per_device(): pl.pallas_call(copy_out, out_shape=[jax.ShapeDtypeStruct(result.shape, re...]
    unnamed x14 -> x0, local copies, waits for them, and re-layouts: 5.96 us -> none
where the time goes in v3:
time: 141 us; the launch traced here: 140 us
  Pallas kernels  140 us (99%)
    pallas_call x1, Pallas kernels, per_device(): pl.pallas_call(functools.partial(kernel, (nodes, inners, chips, width, ff...  124 us
    pallas_call x1, Pallas kernels, per_device(): pl.pallas_call(copy_out, out_shape=[jax.ShapeDtypeStruct(result.shape, re...  15.3 us

profile of v3, /device:TPU:2, one launch (start us, length us, event | category | flops | bytes accessed | tf_op | source)
XLA Modules:
  0.0 140.3 jit_solution(16383888017894827414)
XLA Ops:
  0.6 124.4 %shard_map.118 = (bf16[16,1024]{1,0:T(8,128)(2,1)}, bf16[16,1024]{1,0:T(8,128)(2,1)}, f32[16,10]{1,0:T(8,128)}, bf16[2,128,256]{2,1,0:T(8,128)(2,1)}, bf16[2,128...) custom-call(bf16[16,1024]{1,0:T(8,128)(2,1)} %tokens.1, bf16[16,1024]{1,0:T(8,128)(2,1)} %out_grad.1, ...), custom_call_target="tpu_custom_call" | custom-call | flops 1207959552 | bytes 6291456 | tf_op jit(solution)/shard_map/pallas_call | solution.py:481
  125.0 15.3 %shard_map.119 = (bf16[16,1024]{1,0:T(8,128)(2,1)}, bf16[16,1024]{1,0:T(8,128)(2,1)}, f32[16,10]{1,0:T(8,128)}, bf16[2,128,256]{2,1,0:T(8,128)(2,1)}, bf16[2,128...) custom-call(bf16[16,1024]{1,0:T(8,128)(2,1)} %get-tuple-element.12.refs_0_, bf16[16,1024]{1,0:T(8,128)(2,1)} %get-tuple-element.13.refs_1_, ...), custom_call_target="tpu_custom_call" | custom-call | tf_op jit(solution)/shard_map/pallas_call | solution.py:533

commit v4 on v3

--- a/solution.py
+++ b/solution.py
@@ -17,7 +17,6 @@
 BACK_STRIDE = 3
 ADD_FROM = 4
 ADD_EVERY = 2
-SPLIT = 2
 
 
 def place(distance, nodes):
@@ -206,8 +205,6 @@
             pending.append(copy)
 
     batches = [range(0, chunks // 2), range(chunks // 2, chunks)]
-    if SPLIT == 3 and chunks == 4:
-        batches = [range(0, 2), range(2, 3), range(3, 4)]
     kept = [[] for _ in range(local)]
 
     def of_expert(batch, lanes, e):
@@ -450,14 +447,9 @@
 
 
 def copy_out(*refs):
-    count = (len(refs) - 1) // 2
-    copies = [
-        pltpu.make_async_copy(refs[i], refs[count + i], refs[-1].at[i]) for i in range(count)
-    ]
-    for copy in copies:
-        copy.start()
-    for copy in copies:
-        copy.wait()
+    count = len(refs) // 2
+    for source, target in zip(refs[:count], refs[count:]):
+        target[...] = source[...]
 
 
 def per_device(tokens, out_grad, expert_ids, route_weight, gate_weight, up_weight, down_weight):
@@ -530,12 +522,9 @@
             transcendentals=local * count * ff,
         ),
     )(tokens, out_grad, expert_ids, route_weight, gate_weight, up_weight, down_weight)
+    shapes = [jax.ShapeDtypeStruct(result.shape, result.dtype) for result in results]
     return pl.pallas_call(
-        copy_out,
-        out_shape=[jax.ShapeDtypeStruct(result.shape, result.dtype) for result in results],
-        in_specs=[anywhere] * len(results),
-        out_specs=[anywhere] * len(results),
-        scratch_shapes=[dma((len(results),))],
+        copy_out, out_shape=shapes, in_specs=[vmem] * len(results), out_specs=[vmem] * len(results)
     )(*results)
 
 

time: 141 us -> 127 us (0.901)
  Pallas kernels: 140 us -> 126 us
    pallas_call x1, Pallas kernels: 15.3 us -> 1.86 us  [per_device(): pl.pallas_call(copy_out, out_shape=shapes, in_specs=[vmem] * len(results)...]
where the time goes in v4:
time: 127 us
  Pallas kernels  126 us (99%)
    pallas_call x1, Pallas kernels, per_device(): pl.pallas_call(functools.partial(kernel, (nodes, inners, chips, width, ff...  124 us

profile of v4, /device:TPU:2, one launch (start us, length us, event | category | flops | bytes accessed | tf_op | source)
XLA Modules:
  0.0 126.9 jit_solution(12516929730553840836)
XLA Ops:
  0.6 124.4 %shard_map.118 = (bf16[16,1024]{1,0:T(8,128)(2,1)}, bf16[16,1024]{1,0:T(8,128)(2,1)}, f32[16,10]{1,0:T(8,128)}, bf16[2,128,256]{2,1,0:T(8,128)(2,1)}, bf16[2,128...) custom-call(bf16[16,1024]{1,0:T(8,128)(2,1)} %tokens.1, bf16[16,1024]{1,0:T(8,128)(2,1)} %out_grad.1, ...), custom_call_target="tpu_custom_call" | custom-call | flops 1207959552 | bytes 6291456 | tf_op jit(solution)/shard_map/pallas_call | solution.py:473
  125.0 1.9 %shard_map.119 = (bf16[16,1024]{1,0:T(8,128)(2,1)}, bf16[16,1024]{1,0:T(8,128)(2,1)}, f32[16,10]{1,0:T(8,128)}, bf16[2,128,256]{2,1,0:T(8,128)(2,1)}, bf16[2,128...) custom-call(bf16[16,1024]{1,0:T(8,128)(2,1)} %get-tuple-element.12.refs_0_, bf16[16,1024]{1,0:T(8,128)(2,1)} %get-tuple-element.13.refs_1_, ...), custom_call_target="tpu_custom_call" | custom-call | tf_op jit(solution)/shard_map/pallas_call | solution.py:526

commit v5 on v4

--- a/solution.py
+++ b/solution.py
@@ -204,7 +204,7 @@
             copy.start()
             pending.append(copy)
 
-    batches = [range(0, chunks // 2), range(chunks // 2, chunks)]
+    batches = [range(0, chunks - 1), range(chunks - 1, chunks)]
     kept = [[] for _ in range(local)]
 
     def of_expert(batch, lanes, e):

time: 127 us -> 131 us (1.031)
  Pallas kernels: 126 us -> 130 us
    pallas_call x1, Pallas kernels: 124 us -> 128 us  [per_device(): pl.pallas_call(functools.partial(kernel, (nodes, inners, chips, width, ff...]
where the time goes in v5:
time: 131 us; the launch traced here: 130 us
  Pallas kernels  130 us (99%)
    pallas_call x1, Pallas kernels, per_device(): pl.pallas_call(functools.partial(kernel, (nodes, inners, chips, width, ff...  128 us

profile of v5, /device:TPU:2, one launch (start us, length us, event | category | flops | bytes accessed | tf_op | source)
XLA Modules:
  0.0 130.3 jit_solution(16766435693160909282)
XLA Ops:
  0.6 127.8 %shard_map.118 = (bf16[16,1024]{1,0:T(8,128)(2,1)}, bf16[16,1024]{1,0:T(8,128)(2,1)}, f32[16,10]{1,0:T(8,128)}, bf16[2,128,256]{2,1,0:T(8,128)(2,1)}, bf16[2,128...) custom-call(bf16[16,1024]{1,0:T(8,128)(2,1)} %tokens.1, bf16[16,1024]{1,0:T(8,128)(2,1)} %out_grad.1, ...), custom_call_target="tpu_custom_call" | custom-call | flops 1207959552 | bytes 6291456 | tf_op jit(solution)/shard_map/pallas_call | solution.py:473
  128.5 1.9 %shard_map.119 = (bf16[16,1024]{1,0:T(8,128)(2,1)}, bf16[16,1024]{1,0:T(8,128)(2,1)}, f32[16,10]{1,0:T(8,128)}, bf16[2,128,256]{2,1,0:T(8,128)(2,1)}, bf16[2,128...) custom-call(bf16[16,1024]{1,0:T(8,128)(2,1)} %get-tuple-element.12.refs_0_, bf16[16,1024]{1,0:T(8,128)(2,1)} %get-tuple-element.13.refs_1_, ...), custom_call_target="tpu_custom_call" | custom-call | tf_op jit(solution)/shard_map/pallas_call | solution.py:526
